TPU v7x, 32 devices: a whole 2x2x4 slice. The times are simulated.
32 devices in a mesh: replica: 8 (over y, x, core), fsdp: 4 (over z).
Axes of the slice: x: 2, y: 2, z: 4, core: 2. Of those that a mesh axis runs over, the one named last changes fastest.
Arguments:
- hidden_one: bfloat16 [8192, 7168], P(('replica', 'fsdp')), may hold values from -6 to 6
- hidden_two: bfloat16 [8192, 7168], P(('replica', 'fsdp')), may hold values from -6 to 6
- targets_one: bfloat16 [8192, 512], P(('replica', 'fsdp')), may hold values from -6 to 6
- targets_two: bfloat16 [8192, 512], P(('replica', 'fsdp')), may hold values from -6 to 6
- value_weight: bfloat16 [8, 7168, 512], P('replica', 'fsdp'), may hold values from -6 to 6
- fragment: int32 [1], replicated, may hold values from 0 to 4095
- outer_params: float32 [4, 32, 7168], P(None, 'fsdp'), may hold values from -6 to 6
- outer_momentum: float32 [4, 32, 7168], P(None, 'fsdp'), may hold values from -6 to 6
- local_params: bfloat16 [8, 4, 32, 7168], P('replica', None, 'fsdp'), may hold values from -12 to 12
Outputs:
- new_weight: bfloat16 [8, 7168, 512], P('replica', 'fsdp')
- errors_two: bfloat16 [8192, 512], P(('replica', 'fsdp'))
- merged_params: float32 [32, 7168], P('fsdp')
- merged_momentum: float32 [32, 7168], P('fsdp')
All inputs are finite; a program needn't handle non-finite values.
Results may differ from a plain program's by a relative error of at most 0.009.
Values may be sent and summed in bfloat16 or wider, within the bound.
A program may use at most 128 MiB of HBM per device.

v0:
```python
import jax
import jax.numpy as jnp
from jax import lax
from jax.sharding import PartitionSpec as P

EPS = 1e-06
LEARN_RATE = 0.3
OUTER_RATE = 0.7
MOMENTUM = 0.9


def normalize(rows):
    wide = rows.astype(jnp.float32)
    scale = lax.rsqrt(jnp.mean(wide * wide, axis=1, keepdims=True) + EPS)
    return (wide * scale).astype(jnp.bfloat16)


def rows_adder(normed, piece):
    return jnp.dot(normed, piece, preferred_element_type=jnp.float32)


def block_gradient(columns_all, errors_all, blocks, factor):
    tokens = columns_all.shape[0] // blocks
    parts = columns_all.reshape(blocks, tokens, columns_all.shape[1])
    errs = errors_all.reshape(blocks, tokens, errors_all.shape[1])
    terms = (
        lax.dot_general(
            parts, errs, (((1,), (1,)), ((0,), (0,))), preferred_element_type=jnp.float32
        )
        * factor
    )
    return jnp.sum(terms.astype(jnp.bfloat16).astype(jnp.float32), axis=0)


def per_device(
    hidden_one,
    hidden_two,
    targets_one,
    targets_two,
    value_weight,
    fragment,
    outer_params,
    outer_momentum,
    local_params,
):
    width = hidden_one.shape[1]
    factor = width ** (-0.5)
    blocks = lax.axis_size("fsdp")
    normed_one = normalize(hidden_one)
    normed_two = normalize(hidden_two)
    weight_shard = value_weight[0]
    values_one = (
        rows_adder(normed_one, lax.all_gather(weight_shard, "fsdp", axis=0, tiled=True)) * factor
    )
    errors_one = (values_one - targets_one.astype(jnp.float32)).astype(jnp.bfloat16)
    cols_one = lax.all_to_all(normed_one, "fsdp", split_axis=1, concat_axis=0, tiled=True)
    errs_one = lax.all_gather(errors_one, "fsdp", axis=0, tiled=True)
    grad_one = block_gradient(cols_one, errs_one, blocks, factor)
    next_shard = (weight_shard.astype(jnp.float32) - LEARN_RATE * grad_one).astype(jnp.bfloat16)
    values_two = (
        rows_adder(normed_two, lax.all_gather(next_shard, "fsdp", axis=0, tiled=True)) * factor
    )
    errors_two = (values_two - targets_two.astype(jnp.float32)).astype(jnp.bfloat16)
    cols_two = lax.all_to_all(normed_two, "fsdp", split_axis=1, concat_axis=0, tiled=True)
    errs_two = lax.all_gather(errors_two, "fsdp", axis=0, tiled=True)
    grad_two = block_gradient(cols_two, errs_two, blocks, factor)
    new_shard = (next_shard.astype(jnp.float32) - LEARN_RATE * grad_two).astype(jnp.bfloat16)
    chosen = fragment[0] % outer_params.shape[0]
    params_now = lax.dynamic_index_in_dim(outer_params, chosen, 0, keepdims=False)
    moment_now = lax.dynamic_index_in_dim(outer_momentum, chosen, 0, keepdims=False)
    local_now = lax.dynamic_index_in_dim(local_params[0], chosen, 0, keepdims=False)
    outer_term = params_now - local_now.astype(jnp.float32)
    replicas = lax.axis_size("replica")
    outer_grad = lax.psum(outer_term.astype(jnp.bfloat16), "replica").astype(jnp.float32) / replicas
    merged_momentum = MOMENTUM * moment_now + outer_grad
    merged_params = params_now - OUTER_RATE * (outer_grad + MOMENTUM * merged_momentum)
    return (new_shard[None], errors_two, merged_params, merged_momentum)


def solution(mesh):
    return jax.shard_map(
        per_device,
        mesh=mesh,
        in_specs=(
            P(("replica", "fsdp"), None),
            P(("replica", "fsdp"), None),
            P(("replica", "fsdp"), None),
            P(("replica", "fsdp"), None),
            P("replica", "fsdp", None),
            P(),
            P(None, "fsdp", None),
            P(None, "fsdp", None),
            P("replica", None, "fsdp", None),
        ),
        out_specs=(
            P("replica", "fsdp", None),
            P(("replica", "fsdp"), None),
            P("fsdp", None),
            P("fsdp", None),
        ),
        check_vma=False,
    )
```

profile of v0, /device:TPU:0, one launch (start us, length us, event | category | flops | bytes accessed | tf_op | source)
XLA Modules:
  0.0 523.8 jit_solution(674740286456198658)
XLA Ops:
  8.0 0.0 all-gather.12.cloned.1.call-start
  8.0 0.7 all-gather.12.cloned.1.call-update
  8.7 0.0 copy-start.1
  8.7 3.0 fusion
  11.7 0.1 copy-done.1
  11.9 2.8 fusion.1
  14.6 5.9 %copy.13 = bf16[256,7168]{0,1:T(8,128)(2,1)} copy(bf16[256,7168]{1,0:T(8,128)(2,1)} %fusion.1) | data formatting | bytes 7340032 | tf_op jit(solution)/shard_map/convert_element_type | solution.py:15
  20.5 0.0 copy-start.6
  20.5 6.5 %all-to-all-start = ((bf16[256,4,1792]{0,2,1:T(8,128)(2,1)}), bf16[256,4,1792]{0,2,1:T(8,128)(2,1)}, u32[]{:S(2)}, u32[]{:S(2)}) async-start(bf16[256,4,1792]{0,2,1:T(8,128)(2,1)} %bitcast.52), calls=%async_computation | async-start | bytes 7340032 | tf_op jit(solution)/shard_map/all_to_all | solution.py:56
  27.0 0.0 all-gather.6.cloned.1.call-start
  27.0 196.8 %all-gather.12.cloned.1.call-done = bf16[1,7168,512]{2,1,0:T(8,128)(2,1)} async-done(((bf16[1,1792,512]{2,1,0:T(8,128)(2,1)}), bf16[1,7168,512]{2,1,0:T(8,128)(2,1)}) %all-gather.12.cloned.1.call-update) | async-done | bytes 7340048 | tf_op jit(solution)/shard_map/all_gather | solution.py:53
  223.9 0.0 copy-done.6
  223.9 7.0 %fusion.19 = bf16[256,512]{1,0:T(8,128)(2,1)} fusion(bf16[256,7168]{1,0:T(8,128)(2,1)} %fusion.1, bf16[1,7168,512]{2,1,0:T(8,128)(2,1)} %all-gather.12.cloned.1.call-done, bf16[256,512]{1,0:T(8,128)(2,1)S(1)} %copy-done.6), kind=kOutput, calls=%fused_computation.27 | convolution fusion | flops 1879572480 | bytes 11534336 | tf_op jit(solution)/shard_map/dot_general | solution.py:19
  230.8 0.0 all-gather.6.cloned.1.call-update
  230.9 0.0 all-gather.8.cloned.1.call-start
  230.9 0.0 all-to-all-done
  230.9 26.2 %all-gather.6.cloned.1.call-done = bf16[1024,512]{1,0:T(8,128)(2,1)} async-done(((bf16[256,512]{1,0:T(8,128)(2,1)}), bf16[1024,512]{1,0:T(8,128)(2,1)}) %all-gather.6.cloned.1.call-update) | async-done | bytes 1048592 | tf_op jit(solution)/shard_map/all_gather | solution.py:57
  257.1 0.0 copy-start
  257.1 4.9 convert_reduce_fusion.1
  262.0 0.0 copy-start.3
  262.0 1.9 copy-done.3
  263.9 0.0 copy-done
  263.9 1.9 fusion.8
  265.8 0.0 all-gather.8.cloned.1.call-update
  265.8 0.0 copy-start.2
  265.8 3.0 fusion.2
  268.8 0.1 copy-done.2
  268.9 2.8 fusion.3
  271.7 6.2 %copy.14 = bf16[256,7168]{0,1:T(8,128)(2,1)} copy(bf16[256,7168]{1,0:T(8,128)(2,1)} %fusion.3) | data formatting | bytes 7340032 | tf_op jit(solution)/shard_map/convert_element_type | solution.py:15
  277.9 0.0 copy-start.5
  277.9 0.0 copy-start.7
  277.9 4.9 all-to-all-start.1
  282.8 0.0 all-reduce.2.cloned.1.call-start
  283.5 0.0 copy-done.5
  283.5 1.6 fusion.23
  285.1 0.0 all-reduce.2.cloned.1.call-update
  285.1 0.2 all-gather.10.cloned.1.call-start
  285.3 190.9 %all-gather.8.cloned.1.call-done = bf16[7168,512]{1,0:T(8,128)(2,1)} async-done(((bf16[1792,512]{1,0:T(8,128)(2,1)}), bf16[7168,512]{1,0:T(8,128)(2,1)}) %all-gather.8.cloned.1.call-update) | async-done | bytes 7340048 | tf_op jit(solution)/shard_map/all_gather | solution.py:61
  476.2 0.0 copy-done.7
  476.2 7.0 %fusion.22 = bf16[256,512]{1,0:T(8,128)(2,1)} fusion(bf16[256,7168]{1,0:T(8,128)(2,1)} %fusion.3, bf16[7168,512]{1,0:T(8,128)(2,1)} %all-gather.8.cloned.1.call-done, bf16[256,512]{1,0:T(8,128)(2,1)S(1)} %copy-done.7), kind=kOutput, calls=%fused_computation.28 | convolution fusion | flops 1879572480 | bytes 11534336 | tf_op jit(solution)/shard_map/dot_general | solution.py:19
  483.1 0.0 all-gather.10.cloned.1.call-update
  483.2 0.0 all-reduce.2.cloned.1.call-done
  483.2 1.8 bitcast_subtract_fusion.1
  485.0 0.0 all-to-all-done.1
  485.0 24.4 %all-gather.10.cloned.1.call-done = bf16[1024,512]{1,0:T(8,128)(2,1)} async-done(((bf16[256,512]{1,0:T(8,128)(2,1)}), bf16[1024,512]{1,0:T(8,128)(2,1)}) %all-gather.10.cloned.1.call-update) | async-done | bytes 1048592 | tf_op jit(solution)/shard_map/all_gather | solution.py:65
  509.4 0.0 copy-start.4
  509.4 4.9 convert_reduce_fusion
  514.3 0.0 copy-done.4
  514.3 2.3 fusion.9
  (2 shorter events, 0.0 us)
Async XLA Ops:
  8.0 215.9 %all-gather.12.cloned.1.call-start = ((), (), s32[]{:S(2)}) async-start(), calls=%async_computation.6 | async-start | bytes 9175040 | tf_op jit(solution)/shard_map/all_gather | solution.py:53
  8.7 3.1 copy-start.1
  20.5 203.3 %copy-start.6 = (bf16[256,512]{1,0:T(8,128)(2,1)S(1)}, bf16[256,512]{1,0:T(8,128)(2,1)}, u32[]{:S(2)}) copy-start(bf16[256,512]{1,0:T(8,128)(2,1)} %param.11) | copy-start | bytes 786436
  20.5 210.4 %all-to-all-start = ((bf16[256,4,1792]{0,2,1:T(8,128)(2,1)}), bf16[256,4,1792]{0,2,1:T(8,128)(2,1)}, u32[]{:S(2)}, u32[]{:S(2)}) async-start(bf16[256,4,1792]{0,2,1:T(8,128)(2,1)} %bitcast.52), calls=%async_computation | async-start | bytes 7340032 | tf_op jit(solution)/shard_map/all_to_all | solution.py:56
  27.0 230.1 %all-gather.6.cloned.1.call-start = ((), (), s32[]{:S(2)}) async-start(), calls=%async_computation.2 | async-start | bytes 1310720 | tf_op jit(solution)/shard_map/all_gather | solution.py:57
  230.9 245.3 %all-gather.8.cloned.1.call-start = ((), (), s32[]{:S(2)}) async-start(), calls=%async_computation.3 | async-start | bytes 9175040 | tf_op jit(solution)/shard_map/all_gather | solution.py:61
  257.1 6.8 %copy-start = (bf16[1,1792,512]{2,1,0:T(8,128)(2,1)S(1)}, bf16[1,1792,512]{2,1,0:T(8,128)(2,1)}, u32[]{:S(2)}) copy-start(bf16[1,1792,512]{2,1,0:T(8,128)(2,1)} %param.13) | copy-start | bytes 5505028
  262.0 1.9 copy-start.3
  265.8 3.1 copy-start.2
  277.9 5.6 %copy-start.5 = (f32[4,8,7168]{2,1,0:T(8,128)S(1)}, f32[4,8,7168]{2,1,0:T(8,128)}, u32[]{:S(2)}) copy-start(f32[4,8,7168]{2,1,0:T(8,128)} %param.15) | copy-start | bytes 2752516
  277.9 198.3 %copy-start.7 = (bf16[256,512]{1,0:T(8,128)(2,1)S(1)}, bf16[256,512]{1,0:T(8,128)(2,1)}, u32[]{:S(2)}) copy-start(bf16[256,512]{1,0:T(8,128)(2,1)} %param.12) | copy-start | bytes 786436
  277.9 207.1 %all-to-all-start.1 = ((bf16[256,4,1792]{0,2,1:T(8,128)(2,1)}), bf16[256,4,1792]{0,2,1:T(8,128)(2,1)}, u32[]{:S(2)}, u32[]{:S(2)}) async-start(bf16[256,4,1792]{0,2,1:T(8,128)(2,1)} %bitcast.51), calls=%async_computation.1 | async-start | bytes 7340032 | tf_op jit(solution)/shard_map/all_to_all | solution.py:64
  282.8 200.4 %all-reduce.2.cloned.1.call-start = ((), (), s32[]{:S(2)}) async-start(), calls=%async_computation.5 | async-start | bytes 229376 | tf_op jit(solution)/shard_map/psum | solution.py:74
  285.1 224.3 %all-gather.10.cloned.1.call-start = ((), (), s32[]{:S(2)}) async-start(), calls=%async_computation.4 | async-start | bytes 1310720 | tf_op jit(solution)/shard_map/all_gather | solution.py:65
  509.4 4.9 copy-start.4
Sparse Core Ops, SparseCore 0:
  10.4 213.4 all-gather.11
  231.0 26.0 all-gather.5
  265.9 210.2 all-gather.7
  483.3 26.0 all-gather.9
Sparse Core Ops, SparseCore 1:
  286.9 52.6 all-reduce.1
where the time goes:
time: 524 us
  waiting for transfers between devices  439 us (84%)
  matrix products  23.7 us (5%)
  other arithmetic  19.2 us (4%)
  between operations  16 us (3%)
  local copies, waits for them, and re-layouts  14.2 us (3%)
  starting transfers between devices  11.7 us (2%)
    all_gather x1, waiting for transfers between devices, per_device(): lax.all_gather(weight_shard, 'fsdp', axis=0, tiled=True)  197 us
    all_gather x1, waiting for transfers between devices, per_device(): lax.all_gather(next_shard, 'fsdp', axis=0, tiled=True)  191 us
    all_gather x1, waiting for transfers between devices, per_device(): errs_one = lax.all_gather(errors_one, 'fsdp', axis=0, tiled=True)  26.2 us
    all_gather x1, waiting for transfers between devices, per_device(): errs_two = lax.all_gather(errors_two, 'fsdp', axis=0, tiled=True)  24.4 us
    dot_general x2, matrix products, rows_adder(): return jnp.dot(normed, piece, preferred_element_type=jnp.float32)  13.9 us
    convert_element_type x2, local copies, waits for them, and re-layouts, normalize(): return (wide * scale).astype(jnp.bfloat16)  12 us
  transfers between devices with their start and end apart: 7, of which 4 were waited for; matrix products, arithmetic and copies ran while one was open for 8% of the time, Pallas kernels for 0%

commit v1 on v0

--- a/solution.py
+++ b/solution.py
@@ -15,8 +15,13 @@
     return (wide * scale).astype(jnp.bfloat16)
 
 
-def rows_adder(normed, piece):
-    return jnp.dot(normed, piece, preferred_element_type=jnp.float32)
+def row_sums(columns, shard, factor):
+    part = jnp.dot(columns, shard, preferred_element_type=jnp.float32) * factor
+    pieces = lax.all_to_all(
+        part.astype(jnp.bfloat16), "fsdp", split_axis=0, concat_axis=0, tiled=True
+    )
+    pieces = pieces.reshape(lax.axis_size("fsdp"), -1, part.shape[1])
+    return jnp.sum(pieces.astype(jnp.float32), axis=0)
 
 
 def block_gradient(columns_all, errors_all, blocks, factor):
@@ -25,11 +30,11 @@
     errs = errors_all.reshape(blocks, tokens, errors_all.shape[1])
     terms = (
         lax.dot_general(
-            parts, errs, (((1,), (1,)), ((0,), (0,))), preferred_element_type=jnp.float32
+            parts, errs, (((0, 1), (0, 1)), ((), ())), preferred_element_type=jnp.float32
         )
         * factor
     )
-    return jnp.sum(terms.astype(jnp.bfloat16).astype(jnp.float32), axis=0)
+    return terms
 
 
 def per_device(
@@ -49,19 +54,15 @@
     normed_one = normalize(hidden_one)
     normed_two = normalize(hidden_two)
     weight_shard = value_weight[0]
-    values_one = (
-        rows_adder(normed_one, lax.all_gather(weight_shard, "fsdp", axis=0, tiled=True)) * factor
-    )
+    cols_one = lax.all_to_all(normed_one, "fsdp", split_axis=1, concat_axis=0, tiled=True)
+    cols_two = lax.all_to_all(normed_two, "fsdp", split_axis=1, concat_axis=0, tiled=True)
+    values_one = row_sums(cols_one, weight_shard, factor)
     errors_one = (values_one - targets_one.astype(jnp.float32)).astype(jnp.bfloat16)
-    cols_one = lax.all_to_all(normed_one, "fsdp", split_axis=1, concat_axis=0, tiled=True)
     errs_one = lax.all_gather(errors_one, "fsdp", axis=0, tiled=True)
     grad_one = block_gradient(cols_one, errs_one, blocks, factor)
     next_shard = (weight_shard.astype(jnp.float32) - LEARN_RATE * grad_one).astype(jnp.bfloat16)
-    values_two = (
-        rows_adder(normed_two, lax.all_gather(next_shard, "fsdp", axis=0, tiled=True)) * factor
-    )
+    values_two = row_sums(cols_two, next_shard, factor)
     errors_two = (values_two - targets_two.astype(jnp.float32)).astype(jnp.bfloat16)
-    cols_two = lax.all_to_all(normed_two, "fsdp", split_axis=1, concat_axis=0, tiled=True)
     errs_two = lax.all_gather(errors_two, "fsdp", axis=0, tiled=True)
     grad_two = block_gradient(cols_two, errs_two, blocks, factor)
     new_shard = (next_shard.astype(jnp.float32) - LEARN_RATE * grad_two).astype(jnp.bfloat16)

time: 524 us -> 342 us (0.65)
  waiting for transfers between devices: 439 us -> 245 us
  local copies, waits for them, and re-layouts: 14.2 us -> 23.9 us
  starting transfers between devices: 11.7 us -> 18.5 us
    all_gather x2 -> x0, waiting for transfers between devices: 388 us -> none  [the longest x1 197 us: per_device(): lax.all_gather(weight_shard, 'fsdp', axis=0, tiled=True)]
    all_to_all x1, waiting for transfers between devices: 0.01 us -> 97.3 us  [per_device(): lax.all_to_all(normed_two, 'fsdp', split_axis=1, concat_axis=0, tiled=True)]
    all_to_all x1, waiting for transfers between devices: 0.01 us -> 79.2 us  [per_device(): lax.all_to_all(normed_one, 'fsdp', split_axis=1, concat_axis=0, tiled=True)]
    all_to_all x0 -> x2, waiting for transfers between devices: none -> 37.2 us  [row_sums(): lax.all_to_all(part.astype(jnp.bfloat16), 'fsdp', split_axis=0, concat_ax...]
    psum x1, waiting for transfers between devices: 0.03 us -> 30.8 us  [per_device(): lax.psum(outer_term.astype(jnp.bfloat16), 'replica').astype(jnp.float32)]
    all_gather x1, waiting for transfers between devices: 26.2 us -> 0.01 us  [per_device(): errs_one = lax.all_gather(errors_one, 'fsdp', axis=0, tiled=True)]
    all_gather x1, waiting for transfers between devices: 24.4 us -> 0.01 us  [per_device(): errs_two = lax.all_gather(errors_two, 'fsdp', axis=0, tiled=True)]
    all_to_all x0 -> x2, local copies, waits for them, and re-layouts: none -> 11.9 us  [the longest x1 6.04 us: per_device(): lax.all_to_all(normed_one, 'fsdp', split_axis=1, concat_axis=0, tiled=True)]
  transfers between devices with their start and end apart: 7 -> 7, of which waited for: 4 -> 5; matrix products, arithmetic and copies ran while one was open for 8% -> 7% of each run, Pallas kernels for 0% -> 0%
where the time goes in v1:
time: 342 us; the launch traced here: 341 us
  waiting for transfers between devices  245 us (72%)
  local copies, waits for them, and re-layouts  23.9 us (7%)
  matrix products  19 us (6%)
  other arithmetic  18.7 us (5%)
  starting transfers between devices  18.5 us (5%)
  between operations  16.3 us (5%)
    all_to_all x1, waiting for transfers between devices, per_device(): lax.all_to_all(normed_two, 'fsdp', split_axis=1, concat_axis=0, tiled=True)  97.3 us
    all_to_all x1, waiting for transfers between devices, per_device(): lax.all_to_all(normed_one, 'fsdp', split_axis=1, concat_axis=0, tiled=True)  79.2 us
    all_to_all x2, waiting for transfers between devices, row_sums(): lax.all_to_all(part.astype(jnp.bfloat16), 'fsdp', split_axis=0, concat_ax...  37.2 us
    psum x1, waiting for transfers between devices, per_device(): lax.psum(outer_term.astype(jnp.bfloat16), 'replica').astype(jnp.float32)  30.8 us
    convert_element_type x2, local copies, waits for them, and re-layouts, normalize(): return (wide * scale).astype(jnp.bfloat16)  11.8 us
    dot_general x2, matrix products, block_gradient(): lax.dot_general(parts, errs, (((0, 1), (0, 1)), ((), ())), preferred_elem...  10.9 us
    dot_general x2, matrix products, row_sums(): part = jnp.dot(columns, shard, preferred_element_type=jnp.float32) * factor  8.11 us
    convert_element_type x2, other arithmetic, normalize(): return (wide * scale).astype(jnp.bfloat16)  7.58 us
  transfers between devices with their start and end apart: 7, of which 5 were waited for; matrix products, arithmetic and copies ran while one was open for 7% of the time, Pallas kernels for 0%

profile of v1, /device:TPU:0, one launch (start us, length us, event | category | flops | bytes accessed | tf_op | source)
XLA Modules:
  0.0 340.9 jit_solution(9446254363349953752)
XLA Ops:
  8.0 0.0 copy-start
  8.0 3.0 fusion
  11.0 0.1 copy-done
  11.1 2.8 fusion.1
  13.9 5.9 %copy.15 = bf16[256,7168]{0,1:T(8,128)(2,1)} copy(bf16[256,7168]{1,0:T(8,128)(2,1)} %fusion.1) | data formatting | bytes 7340032 | tf_op jit(solution)/shard_map/convert_element_type | solution.py:15
  19.8 6.3 %all-to-all-start = ((bf16[256,4,1792]{0,2,1:T(8,128)(2,1)}), bf16[256,4,1792]{0,2,1:T(8,128)(2,1)}, u32[]{:S(2)}, u32[]{:S(2)}) async-start(bf16[256,4,1792]{0,2,1:T(8,128)(2,1)} %bitcast.55), calls=%async_computation | async-start | bytes 7340032 | tf_op jit(solution)/shard_map/all_to_all | solution.py:57
  26.2 2.8 fusion.2
  29.0 79.2 %all-to-all-done = bf16[256,4,1792]{0,2,1:T(8,128)(2,1)} async-done(((bf16[256,4,1792]{0,2,1:T(8,128)(2,1)}), bf16[256,4,1792]{0,2,1:T(8,128)(2,1)}, u32[]{:S(2)}, u32[]{:S(2)}) %all-to-all-start) | async-done | bytes 3670048 | tf_op jit(solution)/shard_map/all_to_all | solution.py:57
  108.3 0.0 copy-start.5
  108.3 6.0 %copy.16 = bf16[4,256,1792]{2,1,0:T(8,128)(2,1)} copy(bf16[4,256,1792]{1,2,0:T(8,128)(2,1)} %bitcast.2) | data formatting | bytes 7340032 | tf_op jit(solution)/shard_map/all_to_all | solution.py:57
  114.3 0.0 copy-done.5
  114.3 5.1 %multiply_convert_fusion.1 = bf16[1024,512]{1,0:T(8,128)(2,1)} fusion(bf16[1024,1792]{1,0:T(8,128)(2,1)} %bitcast.57, bf16[1,1792,512]{2,1,0:T(8,128)(2,1)S(1)} %copy-done.5), kind=kOutput, calls=%fused_computation.18 | convolution fusion | flops 1880096768 | bytes 6553600 | tf_op jit(solution)/shard_map/dot_general | solution.py:19
  119.4 3.5 %all-to-all-start.1 = ((bf16[4,256,512]{2,1,0:T(8,128)(2,1)}), bf16[4,256,512]{2,1,0:T(8,128)(2,1)S(1)}, u32[]{:S(2)}, u32[]{:S(2)}) async-start(bf16[4,256,512]{2,1,0:T(8,128)(2,1)} %bitcast.4), calls=%async_computation.1 | async-start | bytes 2097152 | tf_op jit(solution)/shard_map/all_to_all | solution.py:20
  122.9 4.8 %fusion.3 = bf16[256,7168]{1,0:T(8,128)(2,1)} fusion(bf16[256,7168]{1,0:T(8,128)(2,1)} %param.10, f32[256]{0:T(256)S(1)} %add_rsqrt_fusion), kind=kLoop, calls=%fused_computation.7 | loop fusion | flops 5505024 | bytes 7341056 | tf_op jit(solution)/shard_map/convert_element_type | solution.py:15
  127.7 5.9 %copy.17 = bf16[256,7168]{0,1:T(8,128)(2,1)} copy(bf16[256,7168]{1,0:T(8,128)(2,1)} %fusion.3) | data formatting | bytes 7340032 | tf_op jit(solution)/shard_map/convert_element_type | solution.py:15
  133.6 14.4 %all-to-all-done.1 = bf16[4,256,512]{2,1,0:T(8,128)(2,1)S(1)} async-done(((bf16[4,256,512]{2,1,0:T(8,128)(2,1)}), bf16[4,256,512]{2,1,0:T(8,128)(2,1)S(1)}, u32[]{:S(2)}, u32[]{:S(2)}) %all-to-all-start.1) | async-done | bytes 1048608 | tf_op jit(solution)/shard_map/all_to_all | solution.py:20
  148.0 0.0 copy-start.2
  148.0 4.9 %all-to-all-start.2 = ((bf16[256,4,1792]{0,2,1:T(8,128)(2,1)}), bf16[256,4,1792]{0,2,1:T(8,128)(2,1)}, u32[]{:S(2)}, u32[]{:S(2)}) async-start(bf16[256,4,1792]{0,2,1:T(8,128)(2,1)} %bitcast.54), calls=%async_computation.2 | async-start | bytes 7340032 | tf_op jit(solution)/shard_map/all_to_all | solution.py:58
  152.9 0.0 all-gather.3.cloned.1.call-start
  152.9 0.1 convert_reduce_fusion.1
  153.1 0.0 copy-done.2
  153.1 0.8 subtract_convert_fusion.1
  153.9 0.0 all-gather.3.cloned.1.call-update
  153.9 97.3 %all-to-all-done.2 = bf16[256,4,1792]{0,2,1:T(8,128)(2,1)} async-done(((bf16[256,4,1792]{0,2,1:T(8,128)(2,1)}), bf16[256,4,1792]{0,2,1:T(8,128)(2,1)}, u32[]{:S(2)}, u32[]{:S(2)}) %all-to-all-start.2) | async-done | bytes 3670048 | tf_op jit(solution)/shard_map/all_to_all | solution.py:58
  251.2 5.9 %copy.18 = bf16[4,256,1792]{2,1,0:T(8,128)(2,1)} copy(bf16[4,256,1792]{1,2,0:T(8,128)(2,1)} %bitcast.8) | data formatting | bytes 7340032 | tf_op jit(solution)/shard_map/all_to_all | solution.py:58
  257.1 0.0 all-gather.3.cloned.1.call-done
  257.1 0.0 copy-start.1
  257.1 4.6 %fusion.7 = bf16[1792,512]{1,0:T(8,128)(2,1)S(1)} fusion(bf16[4,256,512]{2,1,0:T(8,128)(2,1)} %bitcast.59, bf16[1,1792,512]{2,1,0:T(8,128)(2,1)S(1)} %copy-done.5, bf16[256,4,1792]{0,2,1:T(8,128)(2,1)} %all-to-all-done), kind=kOutput, calls=%fused_computation.13 | convolution fusion | flops 1882718208 | bytes 8388608 | tf_op jit(solution)/shard_map/dot_general | solution.py:32
  261.7 0.0 copy-start.6
  261.7 0.0 copy-done.1
  261.7 0.0 copy-start.4
  261.7 3.1 multiply_convert_fusion
  264.8 0.0 copy-done.6
  264.8 0.0 copy-start.3
  264.8 3.6 %all-to-all-start.3 = ((bf16[4,256,512]{2,1,0:T(8,128)(2,1)}), bf16[4,256,512]{2,1,0:T(8,128)(2,1)S(1)}, u32[]{:S(2)}, u32[]{:S(2)}) async-start(bf16[4,256,512]{2,1,0:T(8,128)(2,1)} %bitcast.10), calls=%async_computation.3 | async-start | bytes 2097152 | tf_op jit(solution)/shard_map/all_to_all | solution.py:20
  268.4 0.0 all-reduce.2.cloned.1.call-start
  269.2 0.0 copy-done.4
  269.2 1.6 fusion.13
  270.7 0.0 all-reduce.2.cloned.1.call-update
  270.8 0.0 all-gather.5.cloned.1.call-start
  270.8 22.8 %all-to-all-done.3 = bf16[4,256,512]{2,1,0:T(8,128)(2,1)S(1)} async-done(((bf16[4,256,512]{2,1,0:T(8,128)(2,1)}), bf16[4,256,512]{2,1,0:T(8,128)(2,1)S(1)}, u32[]{:S(2)}, u32[]{:S(2)}) %all-to-all-start.3) | async-done | bytes 1048608 | tf_op jit(solution)/shard_map/all_to_all | solution.py:20
  293.6 0.1 convert_reduce_fusion
  293.8 0.0 copy-done.3
  293.8 0.8 subtract_convert_fusion
  294.6 0.0 all-gather.5.cloned.1.call-update
  294.6 30.8 %all-reduce.2.cloned.1.call-done = bf16[8,7168]{1,0:T(8,128)(2,1)} async-done(((bf16[8,7168]{1,0:T(8,128)(2,1)}), bf16[8,7168]{1,0:T(8,128)(2,1)}) %all-reduce.2.cloned.1.call-update) | async-done | bytes 114704 | tf_op jit(solution)/shard_map/psum | solution.py:75
  325.3 1.8 bitcast_subtract_fusion
  327.1 0.0 all-gather.5.cloned.1.call-done
  327.1 6.3 %fusion.8 = bf16[1,1792,512]{2,1,0:T(8,128)(2,1)} fusion(bf16[4,256,512]{2,1,0:T(8,128)(2,1)} %bitcast.58, bf16[1792,512]{1,0:T(8,128)(2,1)} %copy-done.6, bf16[256,4,1792]{0,2,1:T(8,128)(2,1)} %all-to-all-done.2), kind=kOutput, calls=%fused_computation.14 | convolution fusion | flops 1882718208 | bytes 8388608 | tf_op jit(solution)/shard_map/dot_general | solution.py:32
  (2 shorter events, 0.0 us)
Async XLA Ops:
  8.0 3.1 copy-start
  19.8 88.4 %all-to-all-start = ((bf16[256,4,1792]{0,2,1:T(8,128)(2,1)}), bf16[256,4,1792]{0,2,1:T(8,128)(2,1)}, u32[]{:S(2)}, u32[]{:S(2)}) async-start(bf16[256,4,1792]{0,2,1:T(8,128)(2,1)} %bitcast.55), calls=%async_computation | async-start | bytes 7340032 | tf_op jit(solution)/shard_map/all_to_all | solution.py:57
  108.3 6.0 %copy-start.5 = (bf16[1,1792,512]{2,1,0:T(8,128)(2,1)S(1)}, bf16[1,1792,512]{2,1,0:T(8,128)(2,1)}, u32[]{:S(2)}) copy-start(bf16[1,1792,512]{2,1,0:T(8,128)(2,1)} %param.13) | copy-start | bytes 5505028
  119.4 28.6 %all-to-all-start.1 = ((bf16[4,256,512]{2,1,0:T(8,128)(2,1)}), bf16[4,256,512]{2,1,0:T(8,128)(2,1)S(1)}, u32[]{:S(2)}, u32[]{:S(2)}) async-start(bf16[4,256,512]{2,1,0:T(8,128)(2,1)} %bitcast.4), calls=%async_computation.1 | async-start | bytes 2097152 | tf_op jit(solution)/shard_map/all_to_all | solution.py:20
  148.0 5.1 %copy-start.2 = (bf16[256,512]{1,0:T(8,128)(2,1)S(1)}, bf16[256,512]{1,0:T(8,128)(2,1)}, u32[]{:S(2)}) copy-start(bf16[256,512]{1,0:T(8,128)(2,1)} %param.11) | copy-start | bytes 786436
  148.0 103.2 %all-to-all-start.2 = ((bf16[256,4,1792]{0,2,1:T(8,128)(2,1)}), bf16[256,4,1792]{0,2,1:T(8,128)(2,1)}, u32[]{:S(2)}, u32[]{:S(2)}) async-start(bf16[256,4,1792]{0,2,1:T(8,128)(2,1)} %bitcast.54), calls=%async_computation.2 | async-start | bytes 7340032 | tf_op jit(solution)/shard_map/all_to_all | solution.py:58
  152.9 104.2 %all-gather.3.cloned.1.call-start = ((), (), s32[]{:S(2)}) async-start(), calls=%async_computation.4 | async-start | bytes 1310720 | tf_op jit(solution)/shard_map/all_gather | solution.py:61
  257.1 4.6 %copy-start.1 = (bf16[4,256,1792]{2,1,0:T(8,128)(2,1)S(1)}, bf16[4,256,1792]{2,1,0:T(8,128)(2,1)}, u32[]{:S(2)}) copy-start(bf16[4,256,1792]{2,1,0:T(8,128)(2,1)} %copy.18) | copy-start | bytes 11010052
  261.7 3.1 copy-start.6
  261.7 7.4 %copy-start.4 = (f32[4,8,7168]{2,1,0:T(8,128)S(1)}, f32[4,8,7168]{2,1,0:T(8,128)}, u32[]{:S(2)}) copy-start(f32[4,8,7168]{2,1,0:T(8,128)} %param.15) | copy-start | bytes 2752516
  264.8 29.0 %copy-start.3 = (bf16[256,512]{1,0:T(8,128)(2,1)S(1)}, bf16[256,512]{1,0:T(8,128)(2,1)}, u32[]{:S(2)}) copy-start(bf16[256,512]{1,0:T(8,128)(2,1)} %param.12) | copy-start | bytes 786436
  264.8 28.8 %all-to-all-start.3 = ((bf16[4,256,512]{2,1,0:T(8,128)(2,1)}), bf16[4,256,512]{2,1,0:T(8,128)(2,1)S(1)}, u32[]{:S(2)}, u32[]{:S(2)}) async-start(bf16[4,256,512]{2,1,0:T(8,128)(2,1)} %bitcast.10), calls=%async_computation.3 | async-start | bytes 2097152 | tf_op jit(solution)/shard_map/all_to_all | solution.py:20
  268.4 56.9 %all-reduce.2.cloned.1.call-start = ((), (), s32[]{:S(2)}) async-start(), calls=%async_computation.6 | async-start | bytes 229376 | tf_op jit(solution)/shard_map/psum | solution.py:75
  270.8 56.4 %all-gather.5.cloned.1.call-start = ((), (), s32[]{:S(2)}) async-start(), calls=%async_computation.5 | async-start | bytes 1310720 | tf_op jit(solution)/shard_map/all_gather | solution.py:66
Sparse Core Ops, SparseCore 0:
  155.9 46.0 all-gather.2
  294.7 27.1 all-gather.4
Sparse Core Ops, SparseCore 1:
  272.5 52.7 all-reduce.1

commit v2 on v0

v2 whole, which is shorter than its diff:
```python
import functools

import jax
import jax.numpy as jnp
from jax import lax
from jax.experimental import pallas as pl
from jax.experimental.pallas import tpu as pltpu
from jax.sharding import PartitionSpec as P

EPS = 1e-06
LEARN_RATE = 0.3
OUTER_RATE = 0.7
MOMENTUM = 0.9
MESH = pl.DeviceIdType.MESH
PIECES = 4
WINDOW = 2


def tile_of(extent):
    return 256 if extent % 256 == 0 else 128


def steps_kernel(
    n,
    h_one,
    h_two,
    t_one,
    t_two,
    w_ref,
    out_w,
    out_e,
    hv,
    xs,
    w_next,
    grad,
    scale,
    vs,
    ra,
    mine,
    rb_out,
    rb_in,
    errs,
    l_sem,
    x_send,
    x_recv,
    a_send,
    a_recv,
    b_send,
    b_recv,
    c_send,
    c_recv,
    i_send,
    i_recv,
    f_send,
    f_recv,
):
    tokens, width = h_one.shape
    cols, feats = w_ref.shape
    tp = tokens // PIECES
    half = n // 2
    factor = width ** (-0.5)
    me = lax.axis_index("fsdp")
    side, spot = me // half, me % half
    other = 1 - side
    cross = other * half + spot
    hidden = (h_one, h_two)
    targets = (t_one, t_two)

    barrier = pltpu.get_barrier_semaphore()
    for d in range(1, n):
        pl.semaphore_signal(
            barrier, inc=1, device_id={"fsdp": lax.rem(me + d, n)}, device_id_type=MESH
        )
    pl.semaphore_wait(barrier, n - 1)

    def remote(src, dst, send, recv, peer):
        return pltpu.make_async_remote_copy(
            src_ref=src,
            dst_ref=dst,
            send_sem=send,
            recv_sem=recv,
            device_id={"fsdp": peer},
            device_id_type=MESH,
        )

    def rows_of(block):
        return pl.ds(pl.multiple_of(block * tp, tp), tp)

    def cols_of(block):
        return pl.ds(pl.multiple_of(block * cols, 128), cols)

    def x_copies(k):
        s, p = k // PIECES, k % PIECES
        out = []
        for d in range(1, n):
            peer = lax.rem(me + d, n)
            out.append(
                remote(
                    hidden[s].at[pl.ds(p * tp, tp), cols_of(peer)],
                    xs.at[s, p, rows_of(me), :],
                    x_send.at[s, p, d - 1],
                    x_recv.at[s, p, d - 1],
                    peer,
                )
            )
        return out

    def half_peers():
        return [(d - 1, side * half + lax.rem(spot + d, half)) for d in range(1, half)]

    def a_copies(s, p):
        return [
            remote(
                vs.at[s, p, :, rows_of(peer - side * half), :],
                ra.at[s, p, d],
                a_send.at[s, p, d],
                a_recv.at[s, p, d],
                peer,
            )
            for d, peer in half_peers()
        ]

    def b_copy(s, p):
        return remote(
            rb_out.at[s, p], rb_in.at[s, p], b_send.at[s, p], b_recv.at[s, p], cross
        )

    def c_copy(s, p):
        piece = errs.at[s, p, rows_of(me), :]
        return remote(piece, piece, c_send.at[s, p], c_recv.at[s, p], cross)

    def i_copies(s, p):
        piece = errs.at[s, p, rows_of(me), :]
        return [
            remote(piece, piece, i_send.at[s, p, d], i_recv.at[s, p, d], peer)
            for d, peer in half_peers()
        ]

    def f_copies(s, p):
        piece = errs.at[s, p, rows_of(cross), :]
        return [
            remote(piece, piece, f_send.at[s, p, d], f_recv.at[s, p, d], peer)
            for d, peer in half_peers()
        ]

    issued = [0]

    def pump():
        k = issued[0]
        if k == 2 * PIECES:
            return
        if k >= WINDOW:
            for copy in x_copies(k - WINDOW):
                copy.wait_send()
        for copy in x_copies(k):
            copy.start()
        issued[0] = k + 1

    for _ in range(WINDOW):
        pump()
    loads = []
    for s in range(2):
        loads.append(pltpu.make_async_copy(hidden[s], hv.at[s], l_sem.at[s, PIECES]))
        for p in range(PIECES):
            loads.append(
                pltpu.make_async_copy(
                    hidden[s].at[pl.ds(p * tp, tp), cols_of(me)],
                    xs.at[s, p, rows_of(me), :],
                    l_sem.at[s, p],
                )
            )
    for copy in loads:
        copy.start()
    for copy in loads:
        copy.wait()
    for s in range(2):

        @pl.loop(0, tokens // 16)
        def _(i):
            rows = pl.ds(pl.multiple_of(i * 16, 16), 16)
            wide = hv[s, rows, :].astype(jnp.float32)
            mean = jnp.sum(wide * wide, axis=1, keepdims=True) * (1.0 / width)
            scale[s, rows, :] = jnp.broadcast_to(lax.rsqrt(mean + EPS), (16, 128))

    def stage_a(s, p):
        weight = w_ref if s == 0 else w_next
        for copy in x_copies(s * PIECES + p):
            copy.wait_recv()
        pump()
        nt = tile_of(feats)

        @pl.loop(0, feats // nt)
        def _(j):
            lanes = pl.ds(pl.multiple_of(j * nt, nt), nt)
            part = jnp.dot(xs[s, p], weight[:, lanes], preferred_element_type=jnp.float32)
            vs[s, p, :, :, lanes] = part.astype(jnp.bfloat16).reshape(2, half * tp, nt)

        for copy in a_copies(s, p):
            copy.start()

    def stage_b(s, p):
        copies = a_copies(s, p)
        for copy in copies:
            copy.wait_recv()
        spots = rows_of(spot)
        away = vs[s, p, other, spots, :].astype(jnp.float32)
        here = vs[s, p, side, spots, :].astype(jnp.float32)
        for d in range(half - 1):
            away = away + ra[s, p, d, other].astype(jnp.float32)
            here = here + ra[s, p, d, side].astype(jnp.float32)
        rb_out[s, p] = away.astype(jnp.bfloat16)
        b_copy(s, p).start()
        mine[s, p] = here

    def stage_c(s, p):
        b_copy(s, p).wait_recv()
        rows = pl.ds(p * tp, tp)
        gain = scale[s, rows, :][:, :1]
        total = mine[s, p] + rb_in[s, p].astype(jnp.float32)
        err = total * (gain * factor) - targets[s][rows, :].astype(jnp.float32)
        err = err.astype(jnp.bfloat16)
        if s == 1:
            out_e[rows, :] = err
        errs[s, p, rows_of(me), :] = (err.astype(jnp.float32) * gain).astype(jnp.bfloat16)
        c_copy(s, p).start()
        for copy in i_copies(s, p):
            copy.start()

    def stage_d(s, p):
        c_copy(s, p).wait_recv()
        for copy in f_copies(s, p):
            copy.start()

    ct = tile_of(cols)

    def stage_f(s, p):
        for copy in i_copies(s, p) + f_copies(s, p):
            copy.wait_recv()
        source = w_ref if s == 0 else w_next
        target = w_next if s == 0 else out_w

        @pl.loop(0, cols // ct)
        def _(j):
            lanes = pl.ds(pl.multiple_of(j * ct, ct), ct)
            term = lax.dot_general(
                xs[s, p, :, lanes],
                errs[s, p],
                (((0,), (0,)), ((), ())),
                preferred_element_type=jnp.float32,
            )
            if p > 0:
                term = grad[lanes, :] + term
            if p < PIECES - 1:
                grad[lanes, :] = term
            else:
                old = source[lanes, :].astype(jnp.float32)
                target[lanes, :] = (old - (LEARN_RATE * factor) * term).astype(jnp.bfloat16)

    stages = (stage_a, stage_b, stage_c, stage_d, stage_f)
    depth = len(stages)
    for s in range(2):
        for t in range(PIECES + depth - 1):
            for lag in range(depth - 1, -1, -1):
                if 0 <= t - lag < PIECES:
                    stages[lag](s, t - lag)
            if t >= PIECES:
                pump()

    for k in range(2 * PIECES - WINDOW, 2 * PIECES):
        for copy in x_copies(k):
            copy.wait_send()
    for s in range(2):
        for p in range(PIECES):
            for copy in a_copies(s, p) + i_copies(s, p) + f_copies(s, p):
                copy.wait_send()
            b_copy(s, p).wait_send()
            c_copy(s, p).wait_send()


def two_steps(hidden_one, hidden_two, targets_one, targets_two, weight):
    n = lax.axis_size("fsdp")
    half = n // 2
    tokens, width = hidden_one.shape
    cols, feats = weight.shape
    tp = tokens // PIECES
    bf, f32 = jnp.bfloat16, jnp.float32
    anywhere = pl.BlockSpec(memory_space=pl.ANY)
    vmem = pl.BlockSpec(memory_space=pltpu.VMEM)
    pair = pltpu.SemaphoreType.DMA((2, PIECES))
    peers = pltpu.SemaphoreType.DMA((2, PIECES, half - 1))
    others = pltpu.SemaphoreType.DMA((2, PIECES, n - 1))
    return pl.pallas_call(
        functools.partial(steps_kernel, n),
        out_shape=(
            jax.ShapeDtypeStruct((cols, feats), bf),
            jax.ShapeDtypeStruct((tokens, feats), bf),
        ),
        in_specs=[anywhere, anywhere, vmem, vmem, vmem],
        out_specs=(vmem, vmem),
        scratch_shapes=[
            pltpu.VMEM((2, tokens, width), bf),
            pltpu.VMEM((2, PIECES, n * tp, cols), bf),
            pltpu.VMEM((cols, feats), bf),
            pltpu.VMEM((cols, feats), f32),
            pltpu.VMEM((2, tokens, 128), f32),
            pltpu.VMEM((2, PIECES, 2, half * tp, feats), bf),
            pltpu.VMEM((2, PIECES, half - 1, 2, tp, feats), bf),
            pltpu.VMEM((2, PIECES, tp, feats), f32),
            pltpu.VMEM((2, PIECES, tp, feats), bf),
            pltpu.VMEM((2, PIECES, tp, feats), bf),
            pltpu.VMEM((2, PIECES, n * tp, feats), bf),
            pltpu.SemaphoreType.DMA((2, PIECES + 1)),
            others,
            others,
            peers,
            peers,
            pair,
            pair,
            pair,
            pair,
            peers,
            peers,
            peers,
            peers,
        ],
        compiler_params=pltpu.CompilerParams(
            collective_id=0, has_side_effects=True, vmem_limit_bytes=56 * 1024 * 1024
        ),
        cost_estimate=pl.CostEstimate(
            flops=8 * n * tokens * cols * feats,
            bytes_accessed=200 * 1024 * 1024,
            transcendentals=0,
        ),
    )(hidden_one, hidden_two, targets_one, targets_two, weight)


def per_device(
    hidden_one,
    hidden_two,
    targets_one,
    targets_two,
    value_weight,
    fragment,
    outer_params,
    outer_momentum,
    local_params,
):
    chosen = fragment[0] % outer_params.shape[0]
    params_now = lax.dynamic_index_in_dim(outer_params, chosen, 0, keepdims=False)
    moment_now = lax.dynamic_index_in_dim(outer_momentum, chosen, 0, keepdims=False)
    local_now = lax.dynamic_index_in_dim(local_params[0], chosen, 0, keepdims=False)
    outer_term = params_now - local_now.astype(jnp.float32)
    replicas = lax.axis_size("replica")
    outer_grad = lax.psum(outer_term.astype(jnp.bfloat16), "replica").astype(jnp.float32) / replicas
    merged_momentum = MOMENTUM * moment_now + outer_grad
    merged_params = params_now - OUTER_RATE * (outer_grad + MOMENTUM * merged_momentum)
    new_shard, errors_two = two_steps(
        hidden_one, hidden_two, targets_one, targets_two, value_weight[0]
    )
    return (new_shard[None], errors_two, merged_params, merged_momentum)


def solution(mesh):
    return jax.shard_map(
        per_device,
        mesh=mesh,
        in_specs=(
            P(("replica", "fsdp"), None),
            P(("replica", "fsdp"), None),
            P(("replica", "fsdp"), None),
            P(("replica", "fsdp"), None),
            P("replica", "fsdp", None),
            P(),
            P(None, "fsdp", None),
            P(None, "fsdp", None),
            P("replica", None, "fsdp", None),
        ),
        out_specs=(
            P("replica", "fsdp", None),
            P(("replica", "fsdp"), None),
            P("fsdp", None),
            P("fsdp", None),
        ),
        check_vma=False,
    )
```

time: 524 us -> 254 us (0.48)
  waiting for transfers between devices: 439 us -> 0.04 us
  Pallas kernels: 0 us -> 231 us
  matrix products: 23.7 us -> 0 us
  other arithmetic: 19.2 us -> 3.62 us
  starting transfers between devices: 11.7 us -> 0.04 us
  local copies, waits for them, and re-layouts: 14.2 us -> 3.59 us
    all_gather x4 -> x0, waiting for transfers between devices: 438 us -> none  [the longest x1 197 us: per_device(): lax.all_gather(weight_shard, 'fsdp', axis=0, tiled=True)]
    pallas_call x0 -> x1, Pallas kernels: none -> 231 us  [two_steps(): pl.pallas_call(functools.partial(steps_kernel, n), out_shape=(jax.ShapeDt...]
    dot_general x4 -> x0, matrix products: 23.7 us -> none  [the longest x2 13.9 us: rows_adder(): return jnp.dot(normed, piece, preferred_element_type=jnp.float32)]
    convert_element_type x2 -> x0, local copies, waits for them, and re-layouts: 12 us -> none  [normalize(): return (wide * scale).astype(jnp.bfloat16)]
    all_to_all x2 -> x0, starting transfers between devices: 11.4 us -> none  [the longest x1 6.5 us: per_device(): lax.all_to_all(normed_one, 'fsdp', split_axis=1, concat_axis=0, tiled=True)]
    convert_element_type x4 -> x0, other arithmetic: 9.76 us -> none  [the longest x2 5.58 us: normalize(): return (wide * scale).astype(jnp.bfloat16)]
    reduce_sum x2 -> x0, other arithmetic: 6 us -> none  [normalize(): scale = lax.rsqrt(jnp.mean(wide * wide, axis=1, keepdims=True) + EPS)]
  transfers between devices with their start and end apart: 7 -> 1, of which waited for: 4 -> 0; matrix products, arithmetic and copies ran while one was open for 8% -> 0% of each run, Pallas kernels for 0% -> 91%
where the time goes in v2:
time: 254 us; the launch traced here: 253 us
  Pallas kernels  231 us (91%)
  between operations  14.7 us (6%)
  other arithmetic  3.62 us (1%)
  local copies, waits for them, and re-layouts  3.59 us (1%)
    pallas_call x1, Pallas kernels, two_steps(): pl.pallas_call(functools.partial(steps_kernel, n), out_shape=(jax.ShapeDt...  231 us
  transfers between devices with their start and end apart: 1, of which 0 were waited for; matrix products, arithmetic and copies ran while one was open for 0% of the time, Pallas kernels for 91%

profile of v2, /device:TPU:0, one launch (start us, length us, event | category | flops | bytes accessed | tf_op | source)
XLA Modules:
  0.0 253.5 jit_solution(15093702969741788876)
XLA Ops:
  7.2 0.0 all-reduce.2.cloned.1.call-start
  7.9 1.7 fusion
  9.6 0.0 all-reduce.2.cloned.1.call-update
  9.6 231.5 %shard_map.120 = (bf16[1792,512]{1,0:T(8,128)(2,1)}, bf16[256,512]{1,0:T(8,128)(2,1)}) custom-call(bf16[256,7168]{1,0:T(8,128)(2,1)} %h_one.1, bf16[256,7168]{1,0:T(8,128)(2,1)} %h_two.1, bf16[256,512]{1,0:T(8,128)(2,1)} %t_one.1, bf16[256,512]{1,0:T(8,128)(2,1)} %t_two.1, bf16[1792,512]{1,0:T(8,128)(2,1)} %bitcast.16), custom_call_target="tpu_custom_call" | custom-call | flops 7516192768 | bytes 209715200 | tf_op jit(solution)/shard_map/pallas_call | solution.py:292
  241.1 0.0 all-reduce.2.cloned.1.call-done
  241.1 1.9 bitcast_subtract_fusion
  243.0 0.0 copy-start
  243.0 2.9 %copy.17 = bf16[1,1792,512]{2,1,0:T(8,128)(2,1)} copy(bf16[1,1792,512]{2,1,0:T(8,128)(2,1)} %bitcast.15) | data formatting | bytes 3670016
  245.9 0.0 copy-done
  245.9 0.7 copy.18
Async XLA Ops:
  7.2 233.9 %all-reduce.2.cloned.1.call-start = ((), (), s32[]{:S(2)}) async-start(), calls=%async_computation | async-start | bytes 229376 | tf_op jit(solution)/shard_map/psum | solution.py:354
  243.0 2.9 %copy-start = (bf16[256,512]{1,0:T(8,128)(2,1)S(1)}, bf16[256,512]{1,0:T(8,128)(2,1)}, u32[]{:S(2)}) copy-start(bf16[256,512]{1,0:T(8,128)(2,1)} %get-tuple-element.15) | copy-start | bytes 786436
Sparse Core Ops, SparseCore 0:
  11.6 54.2 all-reduce.1

commit v3 on v2

--- a/solution.py
+++ b/solution.py
@@ -22,13 +22,28 @@
 
 def steps_kernel(
     n,
+    replicas,
     h_one,
     h_two,
+    t_one_hbm,
+    t_two_hbm,
+    w_hbm,
+    fragment,
+    params_hbm,
+    momentum_hbm,
+    local_hbm,
+    out_w,
+    out_e,
+    out_params,
+    out_momentum,
     t_one,
     t_two,
     w_ref,
-    out_w,
-    out_e,
+    params,
+    momentum,
+    local,
+    outer_sum,
+    outer_in,
     hv,
     xs,
     w_next,
@@ -53,6 +68,9 @@
     i_recv,
     f_send,
     f_recv,
+    o_load,
+    o_send,
+    o_recv,
 ):
     tokens, width = h_one.shape
     cols, feats = w_ref.shape
@@ -66,12 +84,21 @@
     hidden = (h_one, h_two)
     targets = (t_one, t_two)
 
+    mine_r = lax.axis_index("replica")
+    levels = replicas.bit_length() - 1
+    outer_peers = []
+    for k in range(levels):
+        step = 2**k
+        outer_peers.append(mine_r + (1 - 2 * ((mine_r // step) % 2)) * step)
+
     barrier = pltpu.get_barrier_semaphore()
     for d in range(1, n):
         pl.semaphore_signal(
             barrier, inc=1, device_id={"fsdp": lax.rem(me + d, n)}, device_id_type=MESH
         )
-    pl.semaphore_wait(barrier, n - 1)
+    for peer in outer_peers:
+        pl.semaphore_signal(barrier, inc=1, device_id={"replica": peer}, device_id_type=MESH)
+    pl.semaphore_wait(barrier, n - 1 + len(outer_peers))
 
     def remote(src, dst, send, recv, peer):
         return pltpu.make_async_remote_copy(
@@ -169,8 +196,37 @@
                     l_sem.at[s, p],
                 )
             )
-    for copy in loads:
+    outer_loads = []
+    for i, (src, dst) in enumerate(
+        (
+            (params_hbm, params),
+            (local_hbm, local),
+            (momentum_hbm, momentum),
+            (w_hbm, w_ref),
+            (t_one_hbm, t_one),
+            (t_two_hbm, t_two),
+        )
+    ):
+        outer_loads.append(pltpu.make_async_copy(src, dst, o_load.at[i]))
+    for copy in outer_loads + loads:
         copy.start()
+    for copy in outer_loads:
+        copy.wait()
+    chosen = lax.rem(fragment[0], params_hbm.shape[0])
+
+    def outer_copy(k):
+        return pltpu.make_async_remote_copy(
+            src_ref=outer_sum.at[k],
+            dst_ref=outer_in.at[k],
+            send_sem=o_send.at[k],
+            recv_sem=o_recv.at[k],
+            device_id={"replica": outer_peers[k]},
+            device_id_type=MESH,
+        )
+
+    term = params[chosen] - local[chosen].astype(jnp.float32)
+    outer_sum[0] = term.astype(jnp.bfloat16).astype(jnp.float32)
+    outer_copy(0).start()
     for copy in loads:
         copy.wait()
     for s in range(2):
@@ -181,6 +237,20 @@
             wide = hv[s, rows, :].astype(jnp.float32)
             mean = jnp.sum(wide * wide, axis=1, keepdims=True) * (1.0 / width)
             scale[s, rows, :] = jnp.broadcast_to(lax.rsqrt(mean + EPS), (16, 128))
+
+    def outer_level(k):
+        outer_copy(k).wait_recv()
+        total = outer_sum[k] + outer_in[k]
+        if k + 1 < levels:
+            outer_sum[k + 1] = total
+            outer_copy(k + 1).start()
+            return
+        outer_grad = total * (1.0 / replicas)
+        merged = MOMENTUM * momentum[chosen] + outer_grad
+        out_momentum[...] = merged
+        out_params[...] = params[chosen] - OUTER_RATE * (outer_grad + MOMENTUM * merged)
+
+    outer_done = [0]
 
     def stage_a(s, p):
         weight = w_ref if s == 0 else w_next
@@ -265,7 +335,12 @@
                     stages[lag](s, t - lag)
             if t >= PIECES:
                 pump()
-
+            if outer_done[0] < levels:
+                outer_level(outer_done[0])
+                outer_done[0] += 1
+
+    for k in range(levels):
+        outer_copy(k).wait_send()
     for k in range(2 * PIECES - WINDOW, 2 * PIECES):
         for copy in x_copies(k):
             copy.wait_send()
@@ -277,8 +352,22 @@
             c_copy(s, p).wait_send()
 
 
-def two_steps(hidden_one, hidden_two, targets_one, targets_two, weight):
+def per_device(
+    hidden_one,
+    hidden_two,
+    targets_one,
+    targets_two,
+    value_weight,
+    fragment,
+    outer_params,
+    outer_momentum,
+    local_params,
+):
+    weight = value_weight[0]
     n = lax.axis_size("fsdp")
+    replicas = lax.axis_size("replica")
+    levels = replicas.bit_length() - 1
+    frows = outer_params.shape[1]
     half = n // 2
     tokens, width = hidden_one.shape
     cols, feats = weight.shape
@@ -289,15 +378,25 @@
     pair = pltpu.SemaphoreType.DMA((2, PIECES))
     peers = pltpu.SemaphoreType.DMA((2, PIECES, half - 1))
     others = pltpu.SemaphoreType.DMA((2, PIECES, n - 1))
-    return pl.pallas_call(
-        functools.partial(steps_kernel, n),
+    new_shard, errors_two, merged_params, merged_momentum = pl.pallas_call(
+        functools.partial(steps_kernel, n, replicas),
         out_shape=(
             jax.ShapeDtypeStruct((cols, feats), bf),
             jax.ShapeDtypeStruct((tokens, feats), bf),
+            jax.ShapeDtypeStruct((frows, width), f32),
+            jax.ShapeDtypeStruct((frows, width), f32),
         ),
-        in_specs=[anywhere, anywhere, vmem, vmem, vmem],
-        out_specs=(vmem, vmem),
+        in_specs=[anywhere] * 5 + [pl.BlockSpec(memory_space=pltpu.SMEM)] + [anywhere] * 3,
+        out_specs=(vmem, vmem, vmem, vmem),
         scratch_shapes=[
+            pltpu.VMEM((tokens, feats), bf),
+            pltpu.VMEM((tokens, feats), bf),
+            pltpu.VMEM((cols, feats), bf),
+            pltpu.VMEM(outer_params.shape, f32),
+            pltpu.VMEM(outer_params.shape, f32),
+            pltpu.VMEM(local_params.shape[1:], bf),
+            pltpu.VMEM((levels, frows, width), f32),
+            pltpu.VMEM((levels, frows, width), f32),
             pltpu.VMEM((2, tokens, width), bf),
             pltpu.VMEM((2, PIECES, n * tp, cols), bf),
             pltpu.VMEM((cols, feats), bf),
@@ -322,6 +421,9 @@
             peers,
             peers,
             peers,
+            pltpu.SemaphoreType.DMA((6,)),
+            pltpu.SemaphoreType.DMA((levels,)),
+            pltpu.SemaphoreType.DMA((levels,)),
         ],
         compiler_params=pltpu.CompilerParams(
             collective_id=0, has_side_effects=True, vmem_limit_bytes=56 * 1024 * 1024
@@ -331,31 +433,16 @@
             bytes_accessed=200 * 1024 * 1024,
             transcendentals=0,
         ),
-    )(hidden_one, hidden_two, targets_one, targets_two, weight)
-
-
-def per_device(
-    hidden_one,
-    hidden_two,
-    targets_one,
-    targets_two,
-    value_weight,
-    fragment,
-    outer_params,
-    outer_momentum,
-    local_params,
-):
-    chosen = fragment[0] % outer_params.shape[0]
-    params_now = lax.dynamic_index_in_dim(outer_params, chosen, 0, keepdims=False)
-    moment_now = lax.dynamic_index_in_dim(outer_momentum, chosen, 0, keepdims=False)
-    local_now = lax.dynamic_index_in_dim(local_params[0], chosen, 0, keepdims=False)
-    outer_term = params_now - local_now.astype(jnp.float32)
-    replicas = lax.axis_size("replica")
-    outer_grad = lax.psum(outer_term.astype(jnp.bfloat16), "replica").astype(jnp.float32) / replicas
-    merged_momentum = MOMENTUM * moment_now + outer_grad
-    merged_params = params_now - OUTER_RATE * (outer_grad + MOMENTUM * merged_momentum)
-    new_shard, errors_two = two_steps(
-        hidden_one, hidden_two, targets_one, targets_two, value_weight[0]
+    )(
+        hidden_one,
+        hidden_two,
+        targets_one,
+        targets_two,
+        weight,
+        fragment,
+        outer_params,
+        outer_momentum,
+        local_params[0],
     )
     return (new_shard[None], errors_two, merged_params, merged_momentum)
 

time: 254 us -> 236 us (0.929)
  between operations: 14.7 us -> 1.31 us
  other arithmetic: 3.62 us -> 0 us
  transfers between devices with their start and end apart: 1 -> 0, of which waited for: 0 -> 0; matrix products, arithmetic and copies ran while one was open for 0% -> 0% of each run, Pallas kernels for 91% -> 0%
where the time goes in v3:
time: 236 us
  Pallas kernels  230 us (97%)
  local copies, waits for them, and re-layouts  5 us (2%)
    pallas_call x1, Pallas kernels, per_device(): pl.pallas_call(functools.partial(steps_kernel, n, replicas), out_shape=(j...  230 us
    unnamed x10, local copies, waits for them, and re-layouts  5 us

profile of v3, /device:TPU:0, one launch (start us, length us, event | category | flops | bytes accessed | tf_op | source)
XLA Modules:
  0.0 235.9 jit_solution(5502384463412344265)
XLA Ops:
  1.3 229.6 %shard_map.120 = (bf16[1792,512]{1,0:T(8,128)(2,1)}, bf16[256,512]{1,0:T(8,128)(2,1)}, f32[8,7168]{1,0:T(8,128)}, f32[8,7168]{1,0:T(8,128)}) custom-call(bf16[256,7168]{1,0:T(8,128)(2,1)} %h_one.1, bf16[256,7168]{1,0:T(8,128)(2,1)} %h_two.1, bf16[256,512]{1,0:T(8,128)(2,1)} %t_one_hbm.1, bf16[256,512]{1,0:T(8,128)(2,1)} %t_two_hbm.1, ...), custom_call_target="tpu_custom_call" | custom-call | flops 7516192768 | bytes 209715200 | tf_op jit(solution)/shard_map/pallas_call | solution.py:381
  230.9 0.0 copy-start
  230.9 0.0 copy-start.2
  230.9 0.0 copy-start.1
  230.9 2.9 %copy.18 = bf16[1,1792,512]{2,1,0:T(8,128)(2,1)} copy(bf16[1,1792,512]{2,1,0:T(8,128)(2,1)} %bitcast.3) | data formatting | bytes 3670016
  233.8 0.0 copy-done
  233.8 0.7 copy.19
  234.5 0.0 copy-done.2
  234.5 0.7 copy.20
  235.2 0.0 copy-done.1
  235.2 0.7 copy.21
Async XLA Ops:
  230.9 2.9 %copy-start = (bf16[256,512]{1,0:T(8,128)(2,1)S(1)}, bf16[256,512]{1,0:T(8,128)(2,1)}, u32[]{:S(2)}) copy-start(bf16[256,512]{1,0:T(8,128)(2,1)} %get-tuple-element.17) | copy-start | bytes 786436
  230.9 3.6 %copy-start.2 = (f32[8,7168]{1,0:T(8,128)S(1)}, f32[8,7168]{1,0:T(8,128)}, u32[]{:S(2)}) copy-start(f32[8,7168]{1,0:T(8,128)} %get-tuple-element.18) | copy-start | bytes 688132
  230.9 4.3 %copy-start.1 = (f32[8,7168]{1,0:T(8,128)S(1)}, f32[8,7168]{1,0:T(8,128)}, u32[]{:S(2)}) copy-start(f32[8,7168]{1,0:T(8,128)} %get-tuple-element.19) | copy-start | bytes 688132

commit v4 on v3

--- a/solution.py
+++ b/solution.py
@@ -256,7 +256,6 @@
         weight = w_ref if s == 0 else w_next
         for copy in x_copies(s * PIECES + p):
             copy.wait_recv()
-        pump()
         nt = tile_of(feats)
 
         @pl.loop(0, feats // nt)
@@ -267,6 +266,7 @@
 
         for copy in a_copies(s, p):
             copy.start()
+        pump()
 
     def stage_b(s, p):
         copies = a_copies(s, p)
@@ -274,12 +274,13 @@
             copy.wait_recv()
         spots = rows_of(spot)
         away = vs[s, p, other, spots, :].astype(jnp.float32)
+        for d in range(half - 1):
+            away = away + ra[s, p, d, other].astype(jnp.float32)
+        rb_out[s, p] = away.astype(jnp.bfloat16)
+        b_copy(s, p).start()
         here = vs[s, p, side, spots, :].astype(jnp.float32)
         for d in range(half - 1):
-            away = away + ra[s, p, d, other].astype(jnp.float32)
             here = here + ra[s, p, d, side].astype(jnp.float32)
-        rb_out[s, p] = away.astype(jnp.bfloat16)
-        b_copy(s, p).start()
         mine[s, p] = here
 
     def stage_c(s, p):
@@ -330,7 +331,7 @@
     depth = len(stages)
     for s in range(2):
         for t in range(PIECES + depth - 1):
-            for lag in range(depth - 1, -1, -1):
+            for lag in (3, 2, 1, 0, 4):
                 if 0 <= t - lag < PIECES:
                     stages[lag](s, t - lag)
             if t >= PIECES:

time: 236 us -> 236 us (level)
  no operation moved by 1% of the time
where the time goes in v4:
time: 236 us
  Pallas kernels  230 us (97%)
  local copies, waits for them, and re-layouts  5 us (2%)
    pallas_call x1, Pallas kernels, per_device(): pl.pallas_call(functools.partial(steps_kernel, n, replicas), out_shape=(j...  230 us
    unnamed x10, local copies, waits for them, and re-layouts  5 us

profile of v4, /device:TPU:0, one launch (start us, length us, event | category | flops | bytes accessed | tf_op | source)
XLA Modules:
  0.0 236.2 jit_solution(11155872117350693291)
XLA Ops:
  1.3 229.9 %shard_map.120 = (bf16[1792,512]{1,0:T(8,128)(2,1)}, bf16[256,512]{1,0:T(8,128)(2,1)}, f32[8,7168]{1,0:T(8,128)}, f32[8,7168]{1,0:T(8,128)}) custom-call(bf16[256,7168]{1,0:T(8,128)(2,1)} %h_one.1, bf16[256,7168]{1,0:T(8,128)(2,1)} %h_two.1, bf16[256,512]{1,0:T(8,128)(2,1)} %t_one_hbm.1, bf16[256,512]{1,0:T(8,128)(2,1)} %t_two_hbm.1, ...), custom_call_target="tpu_custom_call" | custom-call | flops 7516192768 | bytes 209715200 | tf_op jit(solution)/shard_map/pallas_call | solution.py:382
  231.1 0.0 copy-start
  231.2 0.0 copy-start.2
  231.2 0.0 copy-start.1
  231.2 2.9 %copy.18 = bf16[1,1792,512]{2,1,0:T(8,128)(2,1)} copy(bf16[1,1792,512]{2,1,0:T(8,128)(2,1)} %bitcast.3) | data formatting | bytes 3670016
  234.1 0.0 copy-done
  234.1 0.7 copy.19
  234.8 0.0 copy-done.2
  234.8 0.7 copy.20
  235.5 0.0 copy-done.1
  235.5 0.7 copy.21
Async XLA Ops:
  231.1 2.9 %copy-start = (bf16[256,512]{1,0:T(8,128)(2,1)S(1)}, bf16[256,512]{1,0:T(8,128)(2,1)}, u32[]{:S(2)}) copy-start(bf16[256,512]{1,0:T(8,128)(2,1)} %get-tuple-element.17) | copy-start | bytes 786436
  231.2 3.6 %copy-start.2 = (f32[8,7168]{1,0:T(8,128)S(1)}, f32[8,7168]{1,0:T(8,128)}, u32[]{:S(2)}) copy-start(f32[8,7168]{1,0:T(8,128)} %get-tuple-element.18) | copy-start | bytes 688132
  231.2 4.3 %copy-start.1 = (f32[8,7168]{1,0:T(8,128)S(1)}, f32[8,7168]{1,0:T(8,128)}, u32[]{:S(2)}) copy-start(f32[8,7168]{1,0:T(8,128)} %get-tuple-element.19) | copy-start | bytes 688132
